TPU v7x, 32 devices: a whole 2x2x4 slice. The times are simulated.
32 devices in a mesh: depth: 2 (over y), row: 4 (over x, core), col: 4 (over z).
Axes of the slice: x: 2, y: 2, z: 4, core: 2. Of those that a mesh axis runs over, the one named last changes fastest.
Arguments:
- normed: bfloat16 [1024, 6144], P(('depth', 'col'), 'row'), may hold values from -6 to 6
- positions: int32 [1024], P(('depth', 'col')), may hold values from 0 to 1567, as said below
- cotangent: bfloat16 [1024, 6144], P(('depth', 'col'), 'row'), may hold values from -5 to 5
- w_in: bfloat16 [6144, 12288], P('row', 'col'), may hold values from -0.078125 to 0.078125
- b_in: float32 [12288], P('col'), may hold values from -4 to 4
- w_out: bfloat16 [12288, 6144], P('col', 'row'), may hold values from -0.0546875 to 0.0546875
Outputs:
- d_normed: bfloat16 [1024, 6144], P(('depth', 'col'), 'row')
- d_w_in: float32 [6144, 12288], P('row', 'col')
- d_b_in: float32 [12288], P('col')
- d_w_out: float32 [12288, 6144], P('col', 'row')
Inputs may be any that keep to these rules, and one draw needn't show every extreme that they name: positions holds 4 clips of 256 consecutive tokens; in each clip the same 256 // 8 of the 196 spatial places (ascending, always including places 0 and 195) are kept in each of the 8 frames, position = frame * 196 + place, frames ascending.
All inputs are finite; a program needn't handle non-finite values.
Results may differ from a plain program's by a relative error of at most 0.03.
Values may be sent and summed in bfloat16 or wider, within the bound.
A program may use at most 192 MiB of HBM per device.

v0:
```python
import jax
import jax.numpy as jnp
from jax import lax
from jax.sharding import PartitionSpec as P

D = 6144


coeff = 0.7978845608028654


def sincos(positions, first, width):
    places = positions.astype(jnp.float32)[:, None]
    column = first + jnp.arange(width, dtype=jnp.int32)
    expo = (2 * (column // 2)).astype(jnp.float32) / jnp.float32(D)
    freq = jnp.power(jnp.float32(10000.0), -expo)
    angle = places * freq[None, :]
    return jnp.where((column % 2 == 0)[None, :], jnp.sin(angle), jnp.cos(angle))


def gelu_pair(value):
    inner = coeff * (value + 0.044715 * value * value * value)
    slope = jnp.tanh(inner)
    out = 0.5 * value * (1.0 + slope)
    grad = 0.5 * (1.0 + slope) + 0.5 * value * (1.0 - slope * slope) * coeff * (
        1.0 + 3.0 * 0.044715 * value * value
    )
    return (out, grad)


def on_device(normed, positions, cotangent, w_in, b_in, w_out):
    width = w_in.shape[0]
    first = lax.axis_index("row") * width
    inputs = (normed.astype(jnp.float32) + sincos(positions, first, width)).astype(jnp.bfloat16)
    input_all, cotan_all = (
        lax.all_gather(inputs, "col", axis=0, tiled=True),
        lax.all_gather(cotangent, "col", axis=0, tiled=True),
    )
    rows = input_all
    pre_sum = lax.psum_scatter(
        jnp.dot(rows, w_in, preferred_element_type=jnp.float32).astype(jnp.bfloat16),
        "row",
        scatter_dimension=0,
        tiled=True,
    ).astype(jnp.float32)
    rows = cotan_all
    d_act = lax.psum_scatter(
        lax.dot_general(
            rows, w_out, (((1,), (1,)), ((), ())), preferred_element_type=jnp.float32
        ).astype(jnp.bfloat16),
        "row",
        scatter_dimension=0,
        tiled=True,
    ).astype(jnp.float32)
    pre = pre_sum + b_in[None, :]
    act_f, slope = gelu_pair(pre)
    act = act_f.astype(jnp.bfloat16)
    d_pre = (d_act * slope).astype(jnp.bfloat16)
    act_all, d_pre_all = (
        lax.all_gather(act, "row", axis=0, tiled=True),
        lax.all_gather(d_pre, "row", axis=0, tiled=True),
    )
    rows = d_pre_all
    d_normed = lax.psum_scatter(
        lax.dot_general(
            rows, w_in, (((1,), (1,)), ((), ())), preferred_element_type=jnp.float32
        ).astype(jnp.bfloat16),
        "col",
        scatter_dimension=0,
        tiled=True,
    )
    contract = (((0,), (0,)), ((), ()))
    part_out = lax.dot_general(act_all, cotan_all, contract, preferred_element_type=jnp.float32)
    part_in = lax.dot_general(input_all, d_pre_all, contract, preferred_element_type=jnp.float32)
    part_bias = jnp.sum(d_pre_all.astype(jnp.float32), axis=0)
    d_w_in, d_w_out, d_b_in = (
        lax.psum(part_in.astype(jnp.bfloat16), "depth").astype(jnp.float32),
        lax.psum(part_out.astype(jnp.bfloat16), "depth").astype(jnp.float32),
        lax.psum(part_bias.astype(jnp.bfloat16), "depth").astype(jnp.float32),
    )
    return (d_normed, d_w_in, d_b_in, d_w_out)


def solution(mesh):
    placed = (
        P(("depth", "col"), "row"),
        P(("depth", "col")),
        P(("depth", "col"), "row"),
        P("row", "col"),
        P("col"),
        P("col", "row"),
    )
    return jax.shard_map(
        on_device,
        mesh=mesh,
        in_specs=placed,
        out_specs=(P(("depth", "col"), "row"), P("row", "col"), P("col"), P("col", "row")),
        check_vma=False,
    )
```

profile of v0, /device:TPU:0, one launch (start us, length us, event | category | flops | bytes accessed | tf_op | source)
XLA Modules:
  0.0 714.3 jit_solution(14752643535094820516)
XLA Ops:
  7.3 0.7 convert_element_type.57
  7.9 4.9 fusion.11
  12.8 0.7 all-gather.5.cloned.1.call-update
  13.6 39.1 %all-gather.7.cloned.1.call-done = bf16[512,1536]{1,0:T(8,128)(2,1)} async-done(((bf16[128,1536]{1,0:T(8,128)(2,1)}), bf16[512,1536]{1,0:T(8,128)(2,1)}) %all-gather.7.cloned.1.call-update) | async-done | bytes 1572880 | tf_op jit(solution)/shard_map/all_gather | solution.py:36
  52.7 9.2 %convolution_convert_fusion.2 = bf16[512,3072]{1,0:T(8,128)(2,1)} fusion(bf16[512,1536]{1,0:T(8,128)(2,1)} %all-gather.7.cloned.1.call-done, bf16[1536,3072]{1,0:T(8,128)(2,1)} %param.9), kind=kOutput, calls=%fused_computation.2 | convolution fusion | flops 4833411072 | bytes 14155776 | tf_op jit(solution)/shard_map/dot_general | solution.py:41
  62.0 28.3 %all-gather.5.cloned.1.call-done = bf16[512,1536]{1,0:T(8,128)(2,1)} async-done(((bf16[128,1536]{1,0:T(8,128)(2,1)}), bf16[512,1536]{1,0:T(8,128)(2,1)}) %all-gather.5.cloned.1.call-update) | async-done | bytes 1572880 | tf_op jit(solution)/shard_map/all_gather | solution.py:37
  90.3 9.3 %convolution_convert_fusion.3 = bf16[512,3072]{1,0:T(8,128)(2,1)} fusion(bf16[512,1536]{1,0:T(8,128)(2,1)} %all-gather.5.cloned.1.call-done, bf16[3072,1536]{1,0:T(8,128)(2,1)} %param.11), kind=kOutput, calls=%fused_computation.3 | convolution fusion | flops 4833411072 | bytes 14155776 | tf_op jit(solution)/shard_map/dot_general | solution.py:48
  99.6 30.6 %reduce-scatter.6.cloned.1.call-done = bf16[128,3072]{1,0:T(8,128)(2,1)} async-done(((bf16[512,3072]{1,0:T(8,128)(2,1)}), bf16[128,3072]{1,0:T(8,128)(2,1)}) %reduce-scatter.6.cloned.1.call-update) | async-done | bytes 786448 | tf_op jit(solution)/shard_map/reduce_scatter | solution.py:40
  130.3 41.1 %reduce-scatter.4.cloned.1.call-done = bf16[128,3072]{1,0:T(8,128)(2,1)} async-done(((bf16[512,3072]{1,0:T(8,128)(2,1)}), bf16[128,3072]{1,0:T(8,128)(2,1)}) %reduce-scatter.4.cloned.1.call-update) | async-done | bytes 786448 | tf_op jit(solution)/shard_map/reduce_scatter | solution.py:47
  171.4 3.7 multiply_convert_fusion
  175.2 0.5 all-gather.11.cloned.1.call-update
  175.8 28.1 %all-gather.9.cloned.1.call-done = bf16[512,3072]{1,0:T(8,128)(2,1)} async-done(((bf16[128,3072]{1,0:T(8,128)(2,1)}), bf16[512,3072]{1,0:T(8,128)(2,1)}) %all-gather.9.cloned.1.call-update) | async-done | bytes 3145744 | tf_op jit(solution)/shard_map/all_gather | solution.py:61
  203.8 9.4 %convolution_convert_fusion.1 = bf16[1536,3072]{1,0:T(8,128)(2,1)} fusion(bf16[512,1536]{1,0:T(8,128)(2,1)S(1)} %copy-done.2, bf16[512,3072]{1,0:T(8,128)(2,1)} %all-gather.9.cloned.1.call-done), kind=kOutput, calls=%fused_computation.1 | convolution fusion | flops 4836556800 | bytes 14155776 | tf_op jit(solution)/shard_map/dot_general | solution.py:74
  213.3 21.1 %all-gather.11.cloned.1.call-done = bf16[512,3072]{1,0:T(8,128)(2,1)} async-done(((bf16[128,3072]{1,0:T(8,128)(2,1)}), bf16[512,3072]{1,0:T(8,128)(2,1)}) %all-gather.11.cloned.1.call-update) | async-done | bytes 3145744 | tf_op jit(solution)/shard_map/all_gather | solution.py:60
  234.4 9.4 %convolution_convert_fusion = bf16[3072,1536]{1,0:T(8,128)(2,1)} fusion(bf16[512,3072]{1,0:T(8,128)(2,1)} %all-gather.11.cloned.1.call-done, bf16[512,1536]{1,0:T(8,128)(2,1)S(1)} %copy-done.3), kind=kOutput, calls=%fused_computation | convolution fusion | flops 4836556800 | bytes 14155776 | tf_op jit(solution)/shard_map/dot_general | solution.py:73
  244.1 1.6 copy-done
  245.7 9.0 %convolution_convert_fusion.4 = bf16[512,1536]{1,0:T(8,128)(2,1)} fusion(bf16[512,3072]{1,0:T(8,128)(2,1)S(1)} %copy-done, bf16[1536,3072]{1,0:T(8,128)(2,1)} %param.9), kind=kOutput, calls=%fused_computation.4 | convolution fusion | flops 4832624640 | bytes 14155776 | tf_op jit(solution)/shard_map/dot_general | solution.py:65
  254.7 0.6 reduce_sum.12
  255.3 5.1 psum.22
  260.5 0.6 convert_element_type.66
  261.1 407.0 %all-reduce.3.cloned.1.call-done = (bf16[1536,3072]{1,0:T(8,128)(2,1)}, bf16[3072,1536]{1,0:T(8,128)(2,1)}) async-done(((bf16[1536,3072]{1,0:T(8,128)(2,1)}, bf16[3072,1536]{1,0:T(8,128)(2,1)}), (bf16[1536,3072]{1,0:T(8,128)(2,1)}, bf16[3072,1536]{1,0:T(8,128)(2,1)})) %all-reduce.3.cloned.1.call-update) | async-done | bytes 18874384 | tf_op jit(solution)/shard_map/psum | solution.py:77
  668.1 12.7 %convert_element_type.65 = f32[1536,3072]{1,0:T(8,128)} convert(bf16[1536,3072]{1,0:T(8,128)(2,1)} %get-tuple-element.4) | non-fusion elementwise | flops 4718592 | bytes 28311552 | tf_op jit(solution)/shard_map/convert_element_type | solution.py:77
  680.8 13.2 %convert_element_type.69 = f32[3072,1536]{1,0:T(8,128)} convert(bf16[3072,1536]{1,0:T(8,128)(2,1)} %get-tuple-element.5) | non-fusion elementwise | flops 4718592 | bytes 28311552 | tf_op jit(solution)/shard_map/convert_element_type | solution.py:78
  694.1 13.4 %reduce-scatter.8.cloned.1.call-done = bf16[128,1536]{1,0:T(8,128)(2,1)} async-done(((bf16[512,1536]{1,0:T(8,128)(2,1)}), bf16[128,1536]{1,0:T(8,128)(2,1)}) %reduce-scatter.8.cloned.1.call-update) | async-done | bytes 393232 | tf_op jit(solution)/shard_map/reduce_scatter | solution.py:64
  (23 shorter events, 0.6 us)
Async XLA Ops:
  7.2 45.6 %all-gather.7.cloned.1.call-start = ((), (), s32[]{:S(2)}) async-start(), calls=%async_computation.5 | async-start | bytes 1966080 | tf_op jit(solution)/shard_map/all_gather | solution.py:36
  12.8 77.5 %all-gather.5.cloned.1.call-start = ((), (), s32[]{:S(2)}) async-start(), calls=%async_computation.3 | async-start | bytes 1966080 | tf_op jit(solution)/shard_map/all_gather | solution.py:37
  13.6 116.7 %reduce-scatter.6.cloned.1.call-start = ((), (), s32[]{:S(2)}) async-start(), calls=%async_computation.6 | async-start | bytes 3932160 | tf_op jit(solution)/shard_map/reduce_scatter | solution.py:40
  62.0 109.4 %reduce-scatter.4.cloned.1.call-start = ((), (), s32[]{:S(2)}) async-start(), calls=%async_computation.4 | async-start | bytes 3932160 | tf_op jit(solution)/shard_map/reduce_scatter | solution.py:47
  99.6 71.8 %copy-start.1 = (f32[3072]{0:T(1024)S(1)}, f32[3072]{0:T(1024)}, u32[]{:S(2)}) copy-start(f32[3072]{0:T(1024)} %param.10) | copy-start | bytes 36868
  99.6 104.2 %all-gather.9.cloned.1.call-start = ((), (), s32[]{:S(2)}) async-start(), calls=%async_computation.7 | async-start | bytes 3932160 | tf_op jit(solution)/shard_map/all_gather | solution.py:61
  175.1 28.7 %copy-start.2 = (bf16[512,1536]{1,0:T(8,128)(2,1)S(1)}, bf16[512,1536]{1,0:T(8,128)(2,1)}, u32[]{:S(2)}) copy-start(bf16[512,1536]{1,0:T(8,128)(2,1)} %all-gather.7.cloned.1.call-done) | copy-start | bytes 4718596
  175.1 59.3 %all-gather.11.cloned.1.call-start = ((), (), s32[]{:S(2)}) async-start(), calls=%async_computation.9 | async-start | bytes 3932160 | tf_op jit(solution)/shard_map/all_gather | solution.py:60
  175.7 58.7 %copy-start.3 = (bf16[512,1536]{1,0:T(8,128)(2,1)S(1)}, bf16[512,1536]{1,0:T(8,128)(2,1)}, u32[]{:S(2)}) copy-start(bf16[512,1536]{1,0:T(8,128)(2,1)} %all-gather.5.cloned.1.call-done) | copy-start | bytes 4718596
  175.7 492.4 %all-reduce.3.cloned.1.call-start = ((), (), s32[]{:S(2)}) async-start(), calls=%async_computation.10 | async-start | bytes 37748736 | tf_op jit(solution)/shard_map/psum | solution.py:77
  243.8 1.9 copy-start
  243.8 463.6 %reduce-scatter.8.cloned.1.call-start = ((), (), s32[]{:S(2)}) async-start(), calls=%async_computation.8 | async-start | bytes 1966080 | tf_op jit(solution)/shard_map/reduce_scatter | solution.py:64
Sparse Core Ops, SparseCore 0:
  12.9 39.7 all-gather.6
  54.3 35.9 all-gather.4
  93.4 36.7 reduce-scatter.5
  133.4 37.9 reduce-scatter.3
  175.3 28.5 all-gather.8
  205.8 28.5 all-gather.10
  244.0 424.1 all-reduce.2
  671.1 36.3 reduce-scatter.7
where the time goes:
time: 715 us; the launch traced here: 714 us
  waiting for transfers between devices  610 us (85%)
  matrix products  46.3 us (6%)
  other arithmetic  36.4 us (5%)
  between operations  14.2 us (2%)
    psum x1, waiting for transfers between devices, on_device(): lax.psum(part_in.astype(jnp.bfloat16), 'depth').astype(jnp.float32)  407 us
    reduce_scatter x1, waiting for transfers between devices, on_device(): lax.psum_scatter(lax.dot_general(rows, w_out, (((1,), (1,)), ((), ())), p...  41.1 us
    all_gather x1, waiting for transfers between devices, on_device(): lax.all_gather(inputs, 'col', axis=0, tiled=True)  39.1 us
    reduce_scatter x1, waiting for transfers between devices, on_device(): lax.psum_scatter(jnp.dot(rows, w_in, preferred_element_type=jnp.float32)....  30.6 us
    all_gather x1, waiting for transfers between devices, on_device(): lax.all_gather(cotangent, 'col', axis=0, tiled=True)  28.3 us
    all_gather x1, waiting for transfers between devices, on_device(): lax.all_gather(d_pre, 'row', axis=0, tiled=True)  28.1 us
    all_gather x1, waiting for transfers between devices, on_device(): lax.all_gather(act, 'row', axis=0, tiled=True)  21.1 us
  transfers between devices with their start and end apart: 8, of which 8 were waited for; matrix products, arithmetic and copies ran while one was open for 9% of the time, Pallas kernels for 0%

commit v1 on v0

v1 whole, which is shorter than its diff:
```python
import functools
import math

import jax
import jax.numpy as jnp
from jax import lax
from jax.experimental import pallas as pl
from jax.experimental.pallas import tpu as pltpu
from jax.sharding import PartitionSpec as P

D = 6144
MESH = pl.DeviceIdType.MESH


coeff = 0.7978845608028654


def sincos(positions, first, width):
    places = positions.astype(jnp.float32)[:, None]
    column = first + jnp.arange(width, dtype=jnp.int32)
    expo = (2 * (column // 2)).astype(jnp.float32) / jnp.float32(D)
    freq = jnp.power(jnp.float32(10000.0), -expo)
    angle = places * freq[None, :]
    return jnp.where((column % 2 == 0)[None, :], jnp.sin(angle), jnp.cos(angle))


def gelu_pair(value):
    inner = coeff * (value + 0.044715 * value * value * value)
    slope = jnp.tanh(inner)
    out = 0.5 * value * (1.0 + slope)
    grad = 0.5 * (1.0 + slope) + 0.5 * value * (1.0 - slope * slope) * coeff * (
        1.0 + 3.0 * 0.044715 * value * value
    )
    return (out, grad)


def kernel(
    n_row, n_col,
    x_ref, c_ref, win_ref, wout_ref, b_ref,
    x_all, c_all, a_all, g_all,
    part, half, far,
    s_right, s_left, r_line, s_deep, r_deep,
    s_pair, r_pair, s_far, r_far,
    s_gx, r_gx, s_gy, r_gy, s_gyx, r_gyx, s_sib, r_sib,
):
    d, r, k = lax.axis_index("depth"), lax.axis_index("row"), lax.axis_index("col")
    nx = n_row // 2
    px, core = lax.div(r, 2), lax.rem(r, 2)
    sib = 2 * px + (1 - core)
    other = 1 - d
    block, hidden = x_ref.shape[0], win_ref.shape[1]
    sub = block // n_row
    tile = math.gcd(hidden, 768)
    tiles = hidden // tile
    low = jnp.minimum(k, n_col - 1 - k)
    ins, outs = (x_all, c_all), (a_all, g_all)
    sent = []

    def peer(i):
        return lax.rem(px + i, nx)

    def origin(i):
        return lax.rem(px + nx - i, nx)

    def remote(src, dst, send, recv, **where):
        return pltpu.make_async_remote_copy(
            src_ref=src, dst_ref=dst, send_sem=send, recv_sem=recv,
            device_id=where, device_id_type=MESH,
        )

    def go(*args, **where):
        copy = remote(*args, **where)
        copy.start()
        sent.append(copy)

    def which(s):
        if s == 0:
            return k
        near = k - (s + 1) // 2 if s % 2 else k + s // 2
        rest = jnp.where(2 * k < n_col - 1, k + (s - low), k - (s - low))
        return jnp.where(s <= 2 * low, near, rest)

    def line(arr, b, right):
        ref = ins[arr].at[b]
        if right:
            return remote(ref, ref, s_right.at[arr, b], r_line.at[arr, b], col=jnp.minimum(k + 1, n_col - 1))
        return remote(ref, ref, s_left.at[arr, b], r_line.at[arr, b], col=jnp.maximum(k - 1, 0))

    def deep(arr, b):
        return remote(ins[arr].at[b], ins[arr].at[n_col + b], s_deep.at[arr, b], r_deep.at[arr, b], depth=other)

    def forward(b):
        @pl.when(jnp.logical_and(b <= k, k < n_col - 1))
        def _():
            for arr in (0, 1):
                line(arr, b, True).start()

        @pl.when(jnp.logical_and(b >= k, k > 0))
        def _():
            for arr in (0, 1):
                line(arr, b, False).start()

        for arr in (0, 1):
            deep(arr, b).start()

    def arrive(s):
        b = which(s)
        for arr in (0, 1):
            line(arr, b, True).wait_recv()
        forward(b)

    def project(s):
        b = which(s)
        for arr in (0, 1):

            def body(i, carry):
                cols = pl.ds(pl.multiple_of(i * tile, tile), tile)
                if arr == 0:
                    acc = jnp.dot(x_all[b], win_ref[:, cols], preferred_element_type=jnp.float32)
                else:
                    acc = lax.dot_general(
                        c_all[b], wout_ref[cols, :], (((1,), (1,)), ((), ())),
                        preferred_element_type=jnp.float32,
                    )
                acc = acc.astype(jnp.bfloat16)
                for p in range(nx):
                    for q in (0, 1):
                        at = (2 * p + q) * sub
                        part[s, arr, q, p, :, cols] = acc[at : at + sub]
                return carry

            lax.fori_loop(0, tiles, body, 0)
            go(part.at[s, arr, 1 - core], half.at[s, arr], s_pair.at[s, arr], r_pair.at[s, arr], row=sib)

    def pair_sum(s):
        for arr in (0, 1):
            remote(
                part.at[s, arr, 1 - core], half.at[s, arr], s_pair.at[s, arr], r_pair.at[s, arr], row=sib
            ).wait_recv()

            def body(i, carry):
                cols = pl.ds(pl.multiple_of(i * tile, tile), tile)
                for p in range(nx):
                    mine = part[s, arr, core, p, :, cols].astype(jnp.float32)
                    theirs = half[s, arr, p, :, cols].astype(jnp.float32)
                    half[s, arr, p, :, cols] = (mine + theirs).astype(jnp.bfloat16)
                return carry

            lax.fori_loop(0, tiles, body, 0)
            for i in range(1, nx):
                go(
                    half.at[s, arr, peer(i)], far.at[s, arr, i - 1],
                    s_far.at[s, arr, i - 1], r_far.at[s, arr, i - 1], row=2 * peer(i) + core,
                )

    def finish(s):
        b = which(s)
        for arr in (0, 1):
            for i in range(1, nx):
                remote(
                    half.at[s, arr, peer(i)], far.at[s, arr, i - 1],
                    s_far.at[s, arr, i - 1], r_far.at[s, arr, i - 1], row=2 * peer(i) + core,
                ).wait_recv()

        def body(i, carry):
            cols = pl.ds(pl.multiple_of(i * tile, tile), tile)
            total = []
            for arr in (0, 1):
                value = half[s, arr, px, :, cols].astype(jnp.float32)
                for j in range(1, nx):
                    value = value + far[s, arr, j - 1, :, cols].astype(jnp.float32)
                total.append(value)
            act, slope = gelu_pair(total[0] + b_ref[:, cols])
            a_all[b, r, :, cols] = act.astype(jnp.bfloat16)
            g_all[b, r, :, cols] = (total[1] * slope).astype(jnp.bfloat16)
            return carry

        lax.fori_loop(0, tiles, body, 0)
        for arr in (1, 0):
            own = outs[arr].at[b, r]
            go(own, outs[arr].at[n_col + b, r], s_gy.at[s, arr], r_gy.at[s, arr], depth=other)
        for arr in (1, 0):
            own = outs[arr].at[b, r]
            for i in range(1, nx):
                go(own, own, s_gx.at[s, arr, i - 1], r_gx.at[s, arr, i - 1], row=2 * peer(i) + core)
            go(own, own, s_sib.at[s, arr, 0], r_sib.at[s, arr, 0], row=sib)

    def got(ref, recv):
        remote(ref, ref, s_sib.at[0, 0, 0], recv, row=sib).wait_recv()

    def relay(s):
        b = which(s)
        for arr in (1, 0):
            far_own = outs[arr].at[n_col + b, r]
            got(far_own, r_gy.at[s, arr])
            for i in range(1, nx):
                go(far_own, far_own, s_gyx.at[s, arr, i - 1], r_gyx.at[s, arr, i - 1], row=2 * peer(i) + core)
            go(far_own, far_own, s_sib.at[s, arr, nx], r_sib.at[s, arr, nx], row=sib)
        for arr in (1, 0):
            for i in range(1, nx):
                piece = outs[arr].at[b, 2 * origin(i) + core]
                got(piece, r_gx.at[s, arr, i - 1])
                go(piece, piece, s_sib.at[s, arr, i], r_sib.at[s, arr, i], row=sib)

    def relay_last(s):
        b = which(s)
        for arr in (1, 0):
            for i in range(1, nx):
                piece = outs[arr].at[n_col + b, 2 * origin(i) + core]
                got(piece, r_gyx.at[s, arr, i - 1])
                go(piece, piece, s_sib.at[s, arr, nx + i], r_sib.at[s, arr, nx + i], row=sib)

    barrier = pltpu.get_barrier_semaphore()
    pl.semaphore_signal(barrier, inc=1, device_id={"row": sib}, device_id_type=MESH)
    pl.semaphore_signal(barrier, inc=1, device_id={"depth": other}, device_id_type=MESH)
    for i in range(1, nx):
        pl.semaphore_signal(barrier, inc=1, device_id={"row": 2 * peer(i) + core}, device_id_type=MESH)

    @pl.when(k > 0)
    def _():
        pl.semaphore_signal(barrier, inc=1, device_id={"col": jnp.maximum(k - 1, 0)}, device_id_type=MESH)

    @pl.when(k < n_col - 1)
    def _():
        pl.semaphore_signal(barrier, inc=1, device_id={"col": jnp.minimum(k + 1, n_col - 1)}, device_id_type=MESH)

    x_all[k] = x_ref[...]
    c_all[k] = c_ref[...]
    ends = jnp.where(k > 0, 1, 0) + jnp.where(k < n_col - 1, 1, 0)
    pl.semaphore_wait(barrier, 2 + (nx - 1) + ends)

    forward(k)
    for s in range(n_col):
        if s % 2:
            arrive(s)
            if s + 1 < n_col:
                pl.when(s + 1 <= 2 * low)(functools.partial(arrive, s + 1))
        elif s:
            pl.when(s > 2 * low)(functools.partial(arrive, s))
        project(s)
        if s >= 1:
            finish(s - 1)
        pair_sum(s)
        if s >= 2:
            relay(s - 2)
        if s >= 3:
            relay_last(s - 3)
    finish(n_col - 1)
    for s in range(max(n_col - 2, 0), n_col):
        relay(s)
        if s >= 1:
            relay_last(s - 1)
    relay_last(n_col - 1)

    for s in range(n_col):
        b = which(s)
        for arr in (0, 1):
            for i in range(nx):
                at = 2 * origin(i) + (1 - core)
                got(outs[arr].at[b, at], r_sib.at[s, arr, i])
                got(outs[arr].at[n_col + b, at], r_sib.at[s, arr, nx + i])

    for b in range(n_col):
        for arr in (0, 1):
            deep(arr, b).wait()

            @pl.when(jnp.logical_and(b <= k, k < n_col - 1))
            def _():
                line(arr, b, True).wait_send()

            @pl.when(jnp.logical_and(b >= k, k > 0))
            def _():
                line(arr, b, False).wait_send()

    for copy in sent:
        copy.wait_send()


def exchange(n_row, n_col, inputs, cotangent, w_in, w_out, b_in):
    block, width = inputs.shape
    hidden = w_in.shape[1]
    nx, sub = n_row // 2, block // n_row
    kind = jnp.bfloat16
    wide = jax.ShapeDtypeStruct((2 * n_col, block, width), kind)
    deep = jax.ShapeDtypeStruct((2 * n_col, n_row, sub, hidden), kind)
    vmem = pl.BlockSpec(memory_space=pltpu.VMEM)
    sem = lambda *shape: pltpu.SemaphoreType.DMA(shape)
    flops = 4 * n_col * block * width * hidden
    return pl.pallas_call(
        functools.partial(kernel, n_row, n_col),
        out_shape=(wide, wide, deep, deep),
        in_specs=[vmem] * 5,
        out_specs=(vmem,) * 4,
        scratch_shapes=[
            pltpu.VMEM((n_col, 2, 2, nx, sub, hidden), kind),
            pltpu.VMEM((n_col, 2, nx, sub, hidden), kind),
            pltpu.VMEM((n_col, 2, nx - 1, sub, hidden), kind),
        ]
        + [sem(2, n_col)] * 5
        + [sem(n_col, 2)] * 2
        + [sem(n_col, 2, nx - 1)] * 2
        + [sem(n_col, 2, nx - 1)] * 2
        + [sem(n_col, 2)] * 2
        + [sem(n_col, 2, nx - 1)] * 2
        + [sem(n_col, 2, 2 * nx)] * 2,
        compiler_params=pltpu.CompilerParams(
            collective_id=0, has_side_effects=True, vmem_limit_bytes=60 * 2**20
        ),
        cost_estimate=pl.CostEstimate(
            flops=flops, bytes_accessed=4 * width * hidden, transcendentals=block * hidden
        ),
    )(inputs, cotangent, w_in, w_out, b_in)


def on_device(n_row, n_col, normed, positions, cotangent, w_in, b_in, w_out):
    width, hidden = w_in.shape
    first = lax.axis_index("row") * width
    inputs = (normed.astype(jnp.float32) + sincos(positions, first, width)).astype(jnp.bfloat16)
    x_all, c_all, a_all, g_all = exchange(
        n_row, n_col, inputs, cotangent, w_in, w_out, b_in.reshape(1, hidden)
    )
    rows = x_all.shape[0] * x_all.shape[1]
    grads = g_all.reshape(rows, hidden)
    d_normed = lax.psum_scatter(
        lax.dot_general(
            grads[: rows // 2], w_in, (((1,), (1,)), ((), ())), preferred_element_type=jnp.float32
        ).astype(jnp.bfloat16),
        "col",
        scatter_dimension=0,
        tiled=True,
    )
    contract = (((0,), (0,)), ((), ()))
    d_w_out = lax.dot_general(
        a_all.reshape(rows, hidden), c_all.reshape(rows, width), contract,
        preferred_element_type=jnp.float32,
    )
    d_w_in = lax.dot_general(
        x_all.reshape(rows, width), grads, contract, preferred_element_type=jnp.float32
    )
    d_b_in = jnp.sum(grads.astype(jnp.float32), axis=0)
    return (d_normed, d_w_in, d_b_in, d_w_out)


def solution(mesh):
    placed = (
        P(("depth", "col"), "row"),
        P(("depth", "col")),
        P(("depth", "col"), "row"),
        P("row", "col"),
        P("col"),
        P("col", "row"),
    )
    return jax.shard_map(
        functools.partial(on_device, mesh.shape["row"], mesh.shape["col"]),
        mesh=mesh,
        in_specs=placed,
        out_specs=(P(("depth", "col"), "row"), P("row", "col"), P("col"), P("col", "row")),
        check_vma=False,
    )
```

time: 715 us -> 217 us (0.30)
  waiting for transfers between devices: 610 us -> 1.85 us
  Pallas kernels: 0 us -> 152 us
  other arithmetic: 36.4 us -> 7.07 us
  matrix products: 46.3 us -> 39 us
    psum x1 -> x0, waiting for transfers between devices: 407 us -> none  [on_device(): lax.psum(part_in.astype(jnp.bfloat16), 'depth').astype(jnp.float32)]
    pallas_call x0 -> x1, Pallas kernels: none -> 152 us  [exchange(): pl.pallas_call(functools.partial(kernel, n_row, n_col), out_shape=(wide,...]
    all_gather x4 -> x0, waiting for transfers between devices: 117 us -> none  [the longest x1 39.1 us: on_device(): lax.all_gather(inputs, 'col', axis=0, tiled=True)]
    reduce_scatter x3 -> x1, waiting for transfers between devices: 85.1 us -> 1.83 us  [on_device(): lax.psum_scatter(lax.dot_general(grads[:rows // 2], w_in, (((1,), (1,)),...]
    convert_element_type x4 -> x0, other arithmetic: 30.3 us -> none  [the longest x1 13.2 us: on_device(): lax.psum(part_out.astype(jnp.bfloat16), 'depth').astype(jnp.float32)]
    dot_general x5 -> x3, matrix products: 46.3 us -> 39 us  [the longest x1 17 us: on_device(): lax.dot_general(a_all.reshape(rows, hidden), c_all.reshape(rows, width),...]
  transfers between devices with their start and end apart: 8 -> 1, of which waited for: 8 -> 1; matrix products, arithmetic and copies ran while one was open for 9% -> 15% of each run, Pallas kernels for 0% -> 0%
where the time goes in v1:
time: 217 us
  Pallas kernels  152 us (70%)
  matrix products  39 us (18%)
  between operations  14.1 us (6%)
  other arithmetic  7.07 us (3%)
  local copies, waits for them, and re-layouts  2.48 us (1%)
    pallas_call x1, Pallas kernels, exchange(): pl.pallas_call(functools.partial(kernel, n_row, n_col), out_shape=(wide,...  152 us
    dot_general x1, matrix products, on_device(): lax.dot_general(a_all.reshape(rows, hidden), c_all.reshape(rows, width),...  17 us
    dot_general x1, matrix products, on_device(): lax.dot_general(x_all.reshape(rows, width), grads, contract, preferred_el...  13.1 us
    dot_general x1, matrix products, on_device(): lax.dot_general(grads[:rows // 2], w_in, (((1,), (1,)), ((), ())), prefer...  8.96 us
    convert_element_type x1, other arithmetic, on_device(): (normed.astype(jnp.float32) + sincos(positions, first, width)).astype(jnp...  4.85 us
  transfers between devices with their start and end apart: 1, of which 1 were waited for; matrix products, arithmetic and copies ran while one was open for 15% of the time, Pallas kernels for 0%

profile of v1, /device:TPU:0, one launch (start us, length us, event | category | flops | bytes accessed | tf_op | source)
XLA Modules:
  0.0 216.9 jit_solution(12936685917914032676)
XLA Ops:
  7.2 0.0 reduce-scatter.2.cloned.1.call-start
  7.3 0.7 convert_element_type.24
  7.9 4.9 %fusion.2.x_ref = bf16[128,1536]{1,0:T(8,128)(2,1)} fusion(bf16[128,1536]{1,0:T(8,128)(2,1)} %param.6, f32[1536]{0:T(1024)S(1)} %fusion.8, f32[128]{0:T(128)S(1)} %convert_element_type.24, pred[1536]{0:T(1024)(128)(4,1)S(1)} %fusion.3), kind=kLoop, calls=%fused_computation.6 | loop fusion | flops 983040 | bytes 794624 | tf_op jit(solution)/shard_map/convert_element_type | solution.py:318
  12.8 152.3 %shard_map.93 = (bf16[8,128,1536]{2,1,0:T(8,128)(2,1)}, bf16[8,128,1536]{2,1,0:T(8,128)(2,1)}, bf16[8,4,32,3072]{3,2,1,0:T(8,128)(2,1)}, bf16[8,4,32,3072]{3,2,1,0:T(8,128)(2,1)}) custom-call(bf16[128,1536]{1,0:T(8,128)(2,1)} %fusion.2.x_ref, bf16[128,1536]{1,0:T(8,128)(2,1)} %c_ref.1, bf16[1536,3072]{1,0:T(8,128)(2,1)} %win_ref.1, ...), custom_call_target="tpu_custom_call" | custom-call | flops 9663676416 | bytes 18874368 | tf_op jit(solution)/shard_map/pallas_call | solution.py:289
  165.1 2.1 slice.6
  167.2 9.0 %convolution_convert_fusion = bf16[512,1536]{1,0:T(8,128)(2,1)} fusion(bf16[512,3072]{1,0:T(8,128)(2,1)S(1)} %bitcast.15, bf16[1536,3072]{1,0:T(8,128)(2,1)} %win_ref.1), kind=kOutput, calls=%fused_computation.1 | convolution fusion | flops 4832624640 | bytes 14155776 | tf_op jit(solution)/shard_map/dot_general | solution.py:325
  176.1 0.0 slice-start
  176.1 0.0 reduce-scatter.2.cloned.1.call-update
  176.2 0.0 slice-start.1
  176.2 17.0 %fusion.15 = f32[3072,1536]{1,0:T(8,128)} fusion(bf16[1024,3072]{1,0:T(8,128)(2,1)} %bitcast.17, bf16[1024,1536]{1,0:T(8,128)(2,1)} %bitcast.19), kind=kOutput, calls=%fused_computation.26 | convolution fusion | flops 9663676416 | bytes 28311552 | tf_op jit(solution)/shard_map/dot_general | solution.py:333
  193.1 0.0 slice-done
  193.1 0.0 slice-done.1
  193.1 0.0 copy-start
  193.2 1.5 convert_reduce_fusion
  194.7 0.4 copy-done
  195.1 13.1 %fusion.14 = f32[1536,3072]{1,0:T(8,128)} fusion(bf16[1024,1536]{1,0:T(8,128)(2,1)S(1)} %bitcast.18, bf16[1024,3072]{1,0:T(8,128)(2,1)S(1)} %bitcast.14), kind=kOutput, calls=%fused_computation.25 | convolution fusion | flops 9663676416 | bytes 28311552 | tf_op jit(solution)/shard_map/dot_general | solution.py:337
  208.2 1.8 reduce-scatter.2.cloned.1.call-done
  (3 shorter events, 0.0 us)
Async XLA Ops:
  7.2 202.8 %reduce-scatter.2.cloned.1.call-start = ((), (), s32[]{:S(2)}) async-start(), calls=%async_computation.1 | async-start | bytes 1966080 | tf_op jit(solution)/shard_map/reduce_scatter | solution.py:324
  176.1 17.0 %slice-start = ((s8[6291456]{0:T(1024)(128)(4,1)}), s8[2097152]{0:T(1024)(128)(4,1)S(1)}, s32[]{:S(2)}) async-start(s8[6291456]{0:T(1024)(128)(4,1)} %bitcast.12), calls=%async_computation.2 | async-start | bytes 4194304
  176.2 17.0 %slice-start.1 = ((s8[6291456]{0:T(1024)(128)(4,1)}), s8[4194304]{0:T(1024)(128)(4,1)S(1)}, s32[]{:S(2)}) async-start(s8[6291456]{0:T(1024)(128)(4,1)} %bitcast.12), calls=%async_computation.3 | async-start | bytes 8388608
  193.1 1.9 copy-start
Sparse Core Ops, SparseCore 0:
  176.3 33.6 reduce-scatter.1

commit v2 on v1

--- a/solution.py
+++ b/solution.py
@@ -36,25 +36,40 @@
 
 def kernel(
     n_row, n_col,
-    x_ref, c_ref, win_ref, wout_ref, b_ref,
-    x_all, c_all, a_all, g_all,
-    part, half, far,
+    x_ref, c_ref, win_hbm, wout_hbm, b_ref,
+    x_out, c_out, a_out, g_out, d_out,
+    x_all, c_all, a_all, g_all, win_ref, wout_ref,
+    part, half, far, share, shares,
     s_right, s_left, r_line, s_deep, r_deep,
     s_pair, r_pair, s_far, r_far,
     s_gx, r_gx, s_gy, r_gy, s_gyx, r_gyx, s_sib, r_sib,
+    s_share, r_share, w_sem, o_in, o_mid,
 ):
     d, r, k = lax.axis_index("depth"), lax.axis_index("row"), lax.axis_index("col")
     nx = n_row // 2
     px, core = lax.div(r, 2), lax.rem(r, 2)
     sib = 2 * px + (1 - core)
     other = 1 - d
-    block, hidden = x_ref.shape[0], win_ref.shape[1]
+    block, width = x_ref.shape
+    hidden = win_ref.shape[1]
     sub = block // n_row
     tile = math.gcd(hidden, 768)
     tiles = hidden // tile
     low = jnp.minimum(k, n_col - 1 - k)
     ins, outs = (x_all, c_all), (a_all, g_all)
-    sent = []
+    ins_out, outs_out = (x_out, c_out), (a_out, g_out)
+    sent, kept = [], []
+    weights = [
+        pltpu.make_async_copy(win_hbm, win_ref, w_sem.at[0]),
+        pltpu.make_async_copy(wout_hbm, wout_ref, w_sem.at[1]),
+    ]
+    for copy in weights:
+        copy.start()
+
+    def keep(src, dst, sem):
+        copy = pltpu.make_async_copy(src, dst, sem)
+        copy.start()
+        kept.append(copy)
 
     def peer(i):
         return lax.rem(px + i, nx)
@@ -112,6 +127,8 @@
     def project(s):
         b = which(s)
         for arr in (0, 1):
+            if s == 0:
+                weights[arr].wait()
 
             def body(i, carry):
                 cols = pl.ds(pl.multiple_of(i * tile, tile), tile)
@@ -210,59 +227,92 @@
                 got(piece, r_gyx.at[s, arr, i - 1])
                 go(piece, piece, s_sib.at[s, arr, nx + i], r_sib.at[s, arr, nx + i], row=sib)
 
+    def back(s):
+        b = which(s)
+        for i in range(nx):
+            got(g_all.at[b, 2 * origin(i) + (1 - core)], r_sib.at[s, 1, i])
+        step = math.gcd(width, 768)
+
+        def body(i, carry):
+            cols = pl.ds(pl.multiple_of(i * step, step), step)
+            acc = lax.dot_general(
+                g_all[b].reshape(block, hidden), win_ref[cols, :], (((1,), (1,)), ((), ())),
+                preferred_element_type=jnp.float32,
+            )
+            share[s, :, cols] = acc.astype(jnp.bfloat16)
+            return carry
+
+        lax.fori_loop(0, width // step, body, 0)
+        if s:
+            go(share.at[s], shares.at[k], s_share.at[s], r_share.at[k], col=b)
+
     barrier = pltpu.get_barrier_semaphore()
     pl.semaphore_signal(barrier, inc=1, device_id={"row": sib}, device_id_type=MESH)
     pl.semaphore_signal(barrier, inc=1, device_id={"depth": other}, device_id_type=MESH)
     for i in range(1, nx):
         pl.semaphore_signal(barrier, inc=1, device_id={"row": 2 * peer(i) + core}, device_id_type=MESH)
 
-    @pl.when(k > 0)
-    def _():
-        pl.semaphore_signal(barrier, inc=1, device_id={"col": jnp.maximum(k - 1, 0)}, device_id_type=MESH)
-
-    @pl.when(k < n_col - 1)
-    def _():
-        pl.semaphore_signal(barrier, inc=1, device_id={"col": jnp.minimum(k + 1, n_col - 1)}, device_id_type=MESH)
+    for i in range(1, n_col):
+        pl.semaphore_signal(barrier, inc=1, device_id={"col": lax.rem(k + i, n_col)}, device_id_type=MESH)
 
     x_all[k] = x_ref[...]
     c_all[k] = c_ref[...]
-    ends = jnp.where(k > 0, 1, 0) + jnp.where(k < n_col - 1, 1, 0)
-    pl.semaphore_wait(barrier, 2 + (nx - 1) + ends)
+    pl.semaphore_wait(barrier, 2 + (nx - 1) + (n_col - 1))
 
     forward(k)
     for s in range(n_col):
         if s % 2:
-            arrive(s)
-            if s + 1 < n_col:
-                pl.when(s + 1 <= 2 * low)(functools.partial(arrive, s + 1))
-        elif s:
-            pl.when(s > 2 * low)(functools.partial(arrive, s))
+
+            @pl.when(s <= 2 * low)
+            def _():
+                arrive(s)
+                if s + 1 < n_col:
+                    arrive(s + 1)
+
+        if s >= 1:
+            pl.when(jnp.logical_and(low > 0, s > 2 * low))(functools.partial(arrive, s))
+            finish(s - 1)
+            pl.when(low == 0)(functools.partial(arrive, s))
         project(s)
-        if s >= 1:
-            finish(s - 1)
         pair_sum(s)
         if s >= 2:
-            relay(s - 2)
-        if s >= 3:
-            relay_last(s - 3)
+            back(s - 2)
+        if s >= 1:
+            relay(s - 1)
+        if s >= 2:
+            relay_last(s - 2)
+    for arr in (0, 1):
+        keep(ins[arr].at[pl.ds(0, n_col)], ins_out[arr].at[pl.ds(0, n_col)], o_in.at[arr, n_col])
     finish(n_col - 1)
-    for s in range(max(n_col - 2, 0), n_col):
-        relay(s)
-        if s >= 1:
-            relay_last(s - 1)
+    if n_col >= 2:
+        back(n_col - 2)
+        relay_last(n_col - 2)
+    relay(n_col - 1)
+    back(n_col - 1)
     relay_last(n_col - 1)
 
     for s in range(n_col):
         b = which(s)
-        for arr in (0, 1):
+        for arr in (1, 0):
             for i in range(nx):
                 at = 2 * origin(i) + (1 - core)
-                got(outs[arr].at[b, at], r_sib.at[s, arr, i])
+                if arr == 0:
+                    got(outs[arr].at[b, at], r_sib.at[s, arr, i])
                 got(outs[arr].at[n_col + b, at], r_sib.at[s, arr, nx + i])
+            keep(outs[arr].at[b], outs_out[arr].at[b], o_mid.at[s, arr, 0])
+            keep(outs[arr].at[n_col + b], outs_out[arr].at[n_col + b], o_mid.at[s, arr, 1])
+
+    total = share[0].astype(jnp.float32)
+    for s in range(1, n_col):
+        b = which(s)
+        remote(share.at[s], shares.at[b], s_share.at[s], r_share.at[b], col=b).wait_recv()
+        total = total + shares[b].astype(jnp.float32)
+    d_out[...] = total.astype(jnp.bfloat16)
 
     for b in range(n_col):
         for arr in (0, 1):
             deep(arr, b).wait()
+            keep(ins[arr].at[n_col + b], ins_out[arr].at[n_col + b], o_in.at[arr, b])
 
             @pl.when(jnp.logical_and(b <= k, k < n_col - 1))
             def _():
@@ -274,6 +324,8 @@
 
     for copy in sent:
         copy.wait_send()
+    for copy in kept:
+        copy.wait()
 
 
 def exchange(n_row, n_col, inputs, cotangent, w_in, w_out, b_in):
@@ -283,18 +335,21 @@
     kind = jnp.bfloat16
     wide = jax.ShapeDtypeStruct((2 * n_col, block, width), kind)
     deep = jax.ShapeDtypeStruct((2 * n_col, n_row, sub, hidden), kind)
-    vmem = pl.BlockSpec(memory_space=pltpu.VMEM)
+    vmem, hbm = pl.BlockSpec(memory_space=pltpu.VMEM), pl.BlockSpec(memory_space=pl.ANY)
     sem = lambda *shape: pltpu.SemaphoreType.DMA(shape)
-    flops = 4 * n_col * block * width * hidden
+    flops = 6 * n_col * block * width * hidden
     return pl.pallas_call(
         functools.partial(kernel, n_row, n_col),
-        out_shape=(wide, wide, deep, deep),
-        in_specs=[vmem] * 5,
-        out_specs=(vmem,) * 4,
-        scratch_shapes=[
+        out_shape=(wide, wide, deep, deep, jax.ShapeDtypeStruct((block, width), kind)),
+        in_specs=[vmem, vmem, hbm, hbm, vmem],
+        out_specs=(hbm,) * 4 + (vmem,),
+        scratch_shapes=[pltpu.VMEM(a.shape, kind) for a in (wide, wide, deep, deep, w_in, w_out)]
+        + [
             pltpu.VMEM((n_col, 2, 2, nx, sub, hidden), kind),
             pltpu.VMEM((n_col, 2, nx, sub, hidden), kind),
             pltpu.VMEM((n_col, 2, nx - 1, sub, hidden), kind),
+            pltpu.VMEM((n_col, block, width), kind),
+            pltpu.VMEM((n_col, block, width), kind),
         ]
         + [sem(2, n_col)] * 5
         + [sem(n_col, 2)] * 2
@@ -302,7 +357,9 @@
         + [sem(n_col, 2, nx - 1)] * 2
         + [sem(n_col, 2)] * 2
         + [sem(n_col, 2, nx - 1)] * 2
-        + [sem(n_col, 2, 2 * nx)] * 2,
+        + [sem(n_col, 2, 2 * nx)] * 2
+        + [sem(n_col)] * 2
+        + [sem(2), sem(2, n_col + 1), sem(n_col, 2, 2)],
         compiler_params=pltpu.CompilerParams(
             collective_id=0, has_side_effects=True, vmem_limit_bytes=60 * 2**20
         ),
@@ -316,19 +373,11 @@
     width, hidden = w_in.shape
     first = lax.axis_index("row") * width
     inputs = (normed.astype(jnp.float32) + sincos(positions, first, width)).astype(jnp.bfloat16)
-    x_all, c_all, a_all, g_all = exchange(
+    x_all, c_all, a_all, g_all, d_normed = exchange(
         n_row, n_col, inputs, cotangent, w_in, w_out, b_in.reshape(1, hidden)
     )
     rows = x_all.shape[0] * x_all.shape[1]
     grads = g_all.reshape(rows, hidden)
-    d_normed = lax.psum_scatter(
-        lax.dot_general(
-            grads[: rows // 2], w_in, (((1,), (1,)), ((), ())), preferred_element_type=jnp.float32
-        ).astype(jnp.bfloat16),
-        "col",
-        scatter_dimension=0,
-        tiled=True,
-    )
     contract = (((0,), (0,)), ((), ()))
     d_w_out = lax.dot_general(
         a_all.reshape(rows, hidden), c_all.reshape(rows, width), contract,

time: 217 us -> 198 us (0.912)
  between operations: 14.1 us -> 0.69 us
  matrix products: 39 us -> 29 us
  Pallas kernels: 152 us -> 157 us
  other arithmetic: 7.07 us -> 10 us
    dot_general x1 -> x0, matrix products: 8.96 us -> none  [on_device(): lax.dot_general(grads[:rows // 2], w_in, (((1,), (1,)), ((), ())), prefer...]
    pallas_call x1, Pallas kernels: 152 us -> 157 us  [exchange(): pl.pallas_call(functools.partial(kernel, n_row, n_col), out_shape=(wide,...]
    dot_general x1, matrix products: 17 us -> 13.4 us  [on_device(): lax.dot_general(a_all.reshape(rows, hidden), c_all.reshape(rows, width),...]
    reduce_sum x1, other arithmetic: 1.52 us -> 4.46 us  [on_device(): d_b_in = jnp.sum(grads.astype(jnp.float32), axis=0)]
    dot_general x1, matrix products: 13.1 us -> 15.6 us  [on_device(): lax.dot_general(x_all.reshape(rows, width), grads, contract, preferred_el...]
  transfers between devices with their start and end apart: 1 -> 0, of which waited for: 1 -> 0; matrix products, arithmetic and copies ran while one was open for 15% -> 0% of each run, Pallas kernels for 0% -> 0%
where the time goes in v2:
time: 198 us
  Pallas kernels  157 us (79%)
  matrix products  29 us (15%)
  other arithmetic  10 us (5%)
    pallas_call x1, Pallas kernels, exchange(): pl.pallas_call(functools.partial(kernel, n_row, n_col), out_shape=(wide,...  157 us
    dot_general x1, matrix products, on_device(): lax.dot_general(x_all.reshape(rows, width), grads, contract, preferred_el...  15.6 us
    dot_general x1, matrix products, on_device(): lax.dot_general(a_all.reshape(rows, hidden), c_all.reshape(rows, width),...  13.4 us
    convert_element_type x1, other arithmetic, on_device(): (normed.astype(jnp.float32) + sincos(positions, first, width)).astype(jnp...  4.86 us
    reduce_sum x1, other arithmetic, on_device(): d_b_in = jnp.sum(grads.astype(jnp.float32), axis=0)  4.46 us

profile of v2, /device:TPU:0, one launch (start us, length us, event | category | flops | bytes accessed | tf_op | source)
XLA Modules:
  0.0 197.5 jit_solution(9803144303126010404)
XLA Ops:
  0.6 0.7 convert_element_type.21
  1.3 4.9 %fusion.2.x_ref = bf16[128,1536]{1,0:T(8,128)(2,1)} fusion(bf16[128,1536]{1,0:T(8,128)(2,1)} %param.6, f32[1536]{0:T(1024)S(1)} %fusion.8, f32[128]{0:T(128)S(1)} %convert_element_type.21, pred[1536]{0:T(1024)(128)(4,1)S(1)} %fusion.3), kind=kLoop, calls=%fused_computation.5 | loop fusion | flops 983040 | bytes 794624 | tf_op jit(solution)/shard_map/convert_element_type | solution.py:375
  6.2 156.9 %shard_map.93 = (bf16[8,128,1536]{2,1,0:T(8,128)(2,1)}, bf16[8,128,1536]{2,1,0:T(8,128)(2,1)}, bf16[8,4,32,3072]{3,2,1,0:T(8,128)(2,1)}, bf16[8,4,32,3072]{3,2,1,0:T(8,128)(2,1)}, bf16[128,1536]{1,0:T(8,128)(2,1)}) custom-call(bf16[128,1536]{1,0:T(8,128)(2,1)} %fusion.2.x_ref, bf16[128,1536]{1,0:T(8,128)(2,1)} %c_ref.1, bf16[1536,3072]{1,0:T(8,128)(2,1)} %win_hbm.1, ...), custom_call_target="tpu_custom_call" | custom-call | flops 14495514624 | bytes 18874368 | tf_op jit(solution)/shard_map/pallas_call | solution.py:341
  163.1 0.0 copy-start
  163.1 0.0 slice-start
  163.1 4.5 %convert_reduce_fusion = f32[3072]{0:T(1024)} fusion(bf16[8,4,32,3072]{3,2,1,0:T(8,128)(2,1)} %get-tuple-element.11), kind=kLoop, calls=%fused_computation | loop fusion | flops 6288384 | bytes 6303744 | tf_op jit(solution)/shard_map/reduce_sum | solution.py:389
  167.6 0.1 copy-done
  167.7 0.0 slice-start.1
  167.7 0.0 copy-start.2
  167.7 15.6 %fusion.14 = f32[1536,3072]{1,0:T(8,128)} fusion(bf16[1024,1536]{1,0:T(8,128)(2,1)} %bitcast.15, bf16[1024,3072]{1,0:T(8,128)(2,1)S(1)} %bitcast.9), kind=kOutput, calls=%fused_computation.24 | convolution fusion | flops 9663676416 | bytes 28311552 | tf_op jit(solution)/shard_map/dot_general | solution.py:386
  183.4 0.0 slice-done
  183.4 0.0 slice-done.1
  183.4 0.0 copy-done.2
  183.4 0.0 copy-start.1
  183.4 13.4 %fusion.15 = f32[3072,1536]{1,0:T(8,128)} fusion(bf16[1024,3072]{1,0:T(8,128)(2,1)S(1)} %bitcast.13, bf16[1024,1536]{1,0:T(8,128)(2,1)S(1)} %bitcast.14), kind=kOutput, calls=%fused_computation.25 | convolution fusion | flops 9663676416 | bytes 28311552 | tf_op jit(solution)/shard_map/dot_general | solution.py:382
  196.8 0.0 copy-done.1
  196.8 0.7 copy.11
  (3 shorter events, 0.0 us)
Async XLA Ops:
  163.1 4.6 %copy-start = (bf16[8,4,32,3072]{3,2,1,0:T(8,128)(2,1)S(1)}, bf16[8,4,32,3072]{3,2,1,0:T(8,128)(2,1)}, u32[]{:S(2)}) copy-start(bf16[8,4,32,3072]{3,2,1,0:T(8,128)(2,1)} %get-tuple-element.11) | copy-start | bytes 18874372
  163.1 20.2 %slice-start = ((s8[6291456]{0:T(1024)(128)(4,1)}), s8[4194304]{0:T(1024)(128)(4,1)S(1)}, s32[]{:S(2)}) async-start(s8[6291456]{0:T(1024)(128)(4,1)} %bitcast.11), calls=%async_computation | async-start | bytes 8388608
  167.7 15.6 %slice-start.1 = ((s8[6291456]{0:T(1024)(128)(4,1)}), s8[2097152]{0:T(1024)(128)(4,1)S(1)}, s32[]{:S(2)}) async-start(s8[6291456]{0:T(1024)(128)(4,1)} %bitcast.11), calls=%async_computation.1 | async-start | bytes 4194304
  167.7 15.6 %copy-start.2 = (bf16[8,128,1536]{2,1,0:T(8,128)(2,1)S(1)}, bf16[8,128,1536]{2,1,0:T(8,128)(2,1)}, u32[]{:S(2)}) copy-start(bf16[8,128,1536]{2,1,0:T(8,128)(2,1)} %get-tuple-element.13) | copy-start | bytes 9437188
  183.4 13.4 %copy-start.1 = (bf16[128,1536]{1,0:T(8,128)(2,1)S(1)}, bf16[128,1536]{1,0:T(8,128)(2,1)}, u32[]{:S(2)}) copy-start(bf16[128,1536]{1,0:T(8,128)(2,1)} %get-tuple-element.18) | copy-start | bytes 1179652

commit v3 on v2

--- a/solution.py
+++ b/solution.py
@@ -37,7 +37,7 @@
 def kernel(
     n_row, n_col,
     x_ref, c_ref, win_hbm, wout_hbm, b_ref,
-    x_out, c_out, a_out, g_out, d_out,
+    x_out, c_out, a_out, g_out, d_out, bias,
     x_all, c_all, a_all, g_all, win_ref, wout_ref,
     part, half, far, share, shares,
     s_right, s_left, r_line, s_deep, r_deep,
@@ -115,8 +115,9 @@
             for arr in (0, 1):
                 line(arr, b, False).start()
 
+    def cross(s):
         for arr in (0, 1):
-            deep(arr, b).start()
+            deep(arr, which(s)).start()
 
     def arrive(s):
         b = which(s)
@@ -124,9 +125,9 @@
             line(arr, b, True).wait_recv()
         forward(b)
 
-    def project(s):
-        b = which(s)
-        for arr in (0, 1):
+    def project(s, *arrs):
+        b = which(s)
+        for arr in arrs:
             if s == 0:
                 weights[arr].wait()
 
@@ -227,6 +228,15 @@
                 got(piece, r_gyx.at[s, arr, i - 1])
                 go(piece, piece, s_sib.at[s, arr, nx + i], r_sib.at[s, arr, nx + i], row=sib)
 
+    def add_bias(b):
+        def body(i, carry):
+            cols = pl.ds(pl.multiple_of(i * tile, tile), tile)
+            rows = g_all[b, :, :, cols].astype(jnp.float32).reshape(block, tile)
+            bias[:, cols] += jnp.sum(rows, axis=0, keepdims=True)
+            return carry
+
+        lax.fori_loop(0, tiles, body, 0)
+
     def back(s):
         b = which(s)
         for i in range(nx):
@@ -243,6 +253,7 @@
             return carry
 
         lax.fori_loop(0, width // step, body, 0)
+        add_bias(b)
         if s:
             go(share.at[s], shares.at[k], s_share.at[s], r_share.at[k], col=b)
 
@@ -260,6 +271,8 @@
     pl.semaphore_wait(barrier, 2 + (nx - 1) + (n_col - 1))
 
     forward(k)
+    cross(0)
+    bias[...] = jnp.zeros_like(bias)
     for s in range(n_col):
         if s % 2:
 
@@ -269,16 +282,18 @@
                 if s + 1 < n_col:
                     arrive(s + 1)
 
+        if s:
+            pl.when(s > 2 * low)(functools.partial(arrive, s))
+        project(s, 0)
         if s >= 1:
-            pl.when(jnp.logical_and(low > 0, s > 2 * low))(functools.partial(arrive, s))
             finish(s - 1)
-            pl.when(low == 0)(functools.partial(arrive, s))
-        project(s)
+        project(s, 1)
         pair_sum(s)
         if s >= 2:
             back(s - 2)
         if s >= 1:
             relay(s - 1)
+            cross(s)
         if s >= 2:
             relay_last(s - 2)
     for arr in (0, 1):
@@ -301,6 +316,7 @@
                 got(outs[arr].at[n_col + b, at], r_sib.at[s, arr, nx + i])
             keep(outs[arr].at[b], outs_out[arr].at[b], o_mid.at[s, arr, 0])
             keep(outs[arr].at[n_col + b], outs_out[arr].at[n_col + b], o_mid.at[s, arr, 1])
+        add_bias(n_col + b)
 
     total = share[0].astype(jnp.float32)
     for s in range(1, n_col):
@@ -340,9 +356,9 @@
     flops = 6 * n_col * block * width * hidden
     return pl.pallas_call(
         functools.partial(kernel, n_row, n_col),
-        out_shape=(wide, wide, deep, deep, jax.ShapeDtypeStruct((block, width), kind)),
+        out_shape=(wide, wide, deep, deep, jax.ShapeDtypeStruct((block, width), kind), jax.ShapeDtypeStruct((1, hidden), jnp.float32)),
         in_specs=[vmem, vmem, hbm, hbm, vmem],
-        out_specs=(hbm,) * 4 + (vmem,),
+        out_specs=(hbm,) * 4 + (vmem, vmem),
         scratch_shapes=[pltpu.VMEM(a.shape, kind) for a in (wide, wide, deep, deep, w_in, w_out)]
         + [
             pltpu.VMEM((n_col, 2, 2, nx, sub, hidden), kind),
@@ -373,7 +389,7 @@
     width, hidden = w_in.shape
     first = lax.axis_index("row") * width
     inputs = (normed.astype(jnp.float32) + sincos(positions, first, width)).astype(jnp.bfloat16)
-    x_all, c_all, a_all, g_all, d_normed = exchange(
+    x_all, c_all, a_all, g_all, d_normed, d_b_in = exchange(
         n_row, n_col, inputs, cotangent, w_in, w_out, b_in.reshape(1, hidden)
     )
     rows = x_all.shape[0] * x_all.shape[1]
@@ -386,8 +402,7 @@
     d_w_in = lax.dot_general(
         x_all.reshape(rows, width), grads, contract, preferred_element_type=jnp.float32
     )
-    d_b_in = jnp.sum(grads.astype(jnp.float32), axis=0)
-    return (d_normed, d_w_in, d_b_in, d_w_out)
+    return (d_normed, d_w_in, d_b_in.reshape(hidden), d_w_out)
 
 
 def solution(mesh):

time: 198 us -> 180 us (0.909)
  Pallas kernels: 157 us -> 142 us
  other arithmetic: 10 us -> 5.55 us
    pallas_call x1, Pallas kernels: 157 us -> 142 us  [exchange(): pl.pallas_call(functools.partial(kernel, n_row, n_col), out_shape=(wide,...]
    reduce_sum x1 -> x0, other arithmetic: 4.46 us -> none  [on_device(): d_b_in = jnp.sum(grads.astype(jnp.float32), axis=0)]
where the time goes in v3:
time: 180 us
  Pallas kernels  142 us (79%)
  matrix products  30.6 us (17%)
  other arithmetic  5.55 us (3%)
    pallas_call x1, Pallas kernels, exchange(): pl.pallas_call(functools.partial(kernel, n_row, n_col), out_shape=(wide,...  142 us
    dot_general x1, matrix products, on_device(): lax.dot_general(x_all.reshape(rows, width), grads, contract, preferred_el...  17.2 us
    dot_general x1, matrix products, on_device(): lax.dot_general(a_all.reshape(rows, hidden), c_all.reshape(rows, width),...  13.4 us
    convert_element_type x1, other arithmetic, on_device(): (normed.astype(jnp.float32) + sincos(positions, first, width)).astype(jnp...  4.86 us

profile of v3, /device:TPU:0, one launch (start us, length us, event | category | flops | bytes accessed | tf_op | source)
XLA Modules:
  0.0 179.7 jit_solution(9545065276959432071)
XLA Ops:
  0.6 0.7 convert_element_type.17
  1.3 4.9 %fusion.2.x_ref = bf16[128,1536]{1,0:T(8,128)(2,1)} fusion(bf16[128,1536]{1,0:T(8,128)(2,1)} %param.6, f32[1536]{0:T(1024)S(1)} %fusion.8, f32[128]{0:T(128)S(1)} %convert_element_type.17, pred[1536]{0:T(1024)(128)(4,1)S(1)} %fusion.3), kind=kLoop, calls=%fused_computation.4 | loop fusion | flops 983040 | bytes 794624 | tf_op jit(solution)/shard_map/convert_element_type | solution.py:391
  6.2 141.5 %shard_map.93 = (bf16[8,128,1536]{2,1,0:T(8,128)(2,1)}, bf16[8,128,1536]{2,1,0:T(8,128)(2,1)}, bf16[8,4,32,3072]{3,2,1,0:T(8,128)(2,1)}, bf16[8,4,32,3072]{3,2,1...) custom-call(bf16[128,1536]{1,0:T(8,128)(2,1)} %fusion.2.x_ref, bf16[128,1536]{1,0:T(8,128)(2,1)} %c_ref.1, ...), custom_call_target="tpu_custom_call" | custom-call | flops 14495514624 | bytes 18874368 | tf_op jit(solution)/shard_map/pallas_call | solution.py:357
  147.7 0.0 copy-start.2
  147.8 0.0 copy-start.3
  147.8 17.2 %fusion.14 = f32[1536,3072]{1,0:T(8,128)} fusion(bf16[1024,1536]{1,0:T(8,128)(2,1)} %bitcast.15, bf16[1024,3072]{1,0:T(8,128)(2,1)} %bitcast.13), kind=kOutput, calls=%fused_computation.23 | convolution fusion | flops 9663676416 | bytes 28311552 | tf_op jit(solution)/shard_map/dot_general | solution.py:402
  164.9 0.0 copy-done.2
  164.9 0.0 copy-done.3
  164.9 0.0 copy-start
  164.9 0.0 copy-start.1
  164.9 13.4 %fusion.15 = f32[3072,1536]{1,0:T(8,128)} fusion(bf16[1024,3072]{1,0:T(8,128)(2,1)S(1)} %bitcast.12, bf16[1024,1536]{1,0:T(8,128)(2,1)S(1)} %bitcast.14), kind=kOutput, calls=%fused_computation.24 | convolution fusion | flops 9663676416 | bytes 28311552 | tf_op jit(solution)/shard_map/dot_general | solution.py:398
  178.4 0.0 copy-done
  178.4 0.7 copy.12
  179.1 0.0 copy-done.1
  179.1 0.6 copy.13
  (2 shorter events, 0.0 us)
Async XLA Ops:
  147.7 17.2 %copy-start.2 = (bf16[8,4,32,3072]{3,2,1,0:T(8,128)(2,1)S(1)}, bf16[8,4,32,3072]{3,2,1,0:T(8,128)(2,1)}, u32[]{:S(2)}) copy-start(bf16[8,4,32,3072]{3,2,1,0:T(8,128)(2,1)} %get-tuple-element.14) | copy-start | bytes 18874372
  147.8 17.2 %copy-start.3 = (bf16[8,128,1536]{2,1,0:T(8,128)(2,1)S(1)}, bf16[8,128,1536]{2,1,0:T(8,128)(2,1)}, u32[]{:S(2)}) copy-start(bf16[8,128,1536]{2,1,0:T(8,128)(2,1)} %get-tuple-element.15) | copy-start | bytes 9437188
  164.9 13.5 %copy-start = (bf16[128,1536]{1,0:T(8,128)(2,1)S(1)}, bf16[128,1536]{1,0:T(8,128)(2,1)}, u32[]{:S(2)}) copy-start(bf16[128,1536]{1,0:T(8,128)(2,1)} %get-tuple-element.20) | copy-start | bytes 1179652
  164.9 14.2 %copy-start.1 = (f32[1,3072]{1,0:T(1,128)S(1)}, f32[1,3072]{1,0:T(1,128)}, u32[]{:S(2)}) copy-start(f32[1,3072]{1,0:T(1,128)} %get-tuple-element.13) | copy-start | bytes 36868

commit v4 on v3

--- a/solution.py
+++ b/solution.py
@@ -150,8 +150,8 @@
             lax.fori_loop(0, tiles, body, 0)
             go(part.at[s, arr, 1 - core], half.at[s, arr], s_pair.at[s, arr], r_pair.at[s, arr], row=sib)
 
-    def pair_sum(s):
-        for arr in (0, 1):
+    def pair_sum(s, *arrs):
+        for arr in arrs:
             remote(
                 part.at[s, arr, 1 - core], half.at[s, arr], s_pair.at[s, arr], r_pair.at[s, arr], row=sib
             ).wait_recv()
@@ -287,8 +287,11 @@
         project(s, 0)
         if s >= 1:
             finish(s - 1)
+            pair_sum(s, 0)
         project(s, 1)
-        pair_sum(s)
+        if s == 0:
+            pair_sum(s, 0)
+        pair_sum(s, 1)
         if s >= 2:
             back(s - 2)
         if s >= 1:

time: 180 us -> 180 us (level)
  no operation moved by 1% of the time
where the time goes in v4:
time: 180 us
  Pallas kernels  142 us (79%)
  matrix products  30.6 us (17%)
  other arithmetic  5.55 us (3%)
    pallas_call x1, Pallas kernels, exchange(): pl.pallas_call(functools.partial(kernel, n_row, n_col), out_shape=(wide,...  142 us
    dot_general x1, matrix products, on_device(): lax.dot_general(x_all.reshape(rows, width), grads, contract, preferred_el...  17.2 us
    dot_general x1, matrix products, on_device(): lax.dot_general(a_all.reshape(rows, hidden), c_all.reshape(rows, width),...  13.4 us
    convert_element_type x1, other arithmetic, on_device(): (normed.astype(jnp.float32) + sincos(positions, first, width)).astype(jnp...  4.86 us

profile of v4, /device:TPU:0, one launch (start us, length us, event | category | flops | bytes accessed | tf_op | source)
XLA Modules:
  0.0 179.7 jit_solution(4970942416054910996)
XLA Ops:
  0.6 0.7 convert_element_type.17
  1.3 4.9 %fusion.2.x_ref = bf16[128,1536]{1,0:T(8,128)(2,1)} fusion(bf16[128,1536]{1,0:T(8,128)(2,1)} %param.6, f32[1536]{0:T(1024)S(1)} %fusion.8, f32[128]{0:T(128)S(1)} %convert_element_type.17, pred[1536]{0:T(1024)(128)(4,1)S(1)} %fusion.3), kind=kLoop, calls=%fused_computation.4 | loop fusion | flops 983040 | bytes 794624 | tf_op jit(solution)/shard_map/convert_element_type | solution.py:394
  6.2 141.5 %shard_map.93 = (bf16[8,128,1536]{2,1,0:T(8,128)(2,1)}, bf16[8,128,1536]{2,1,0:T(8,128)(2,1)}, bf16[8,4,32,3072]{3,2,1,0:T(8,128)(2,1)}, bf16[8,4,32,3072]{3,2,1...) custom-call(bf16[128,1536]{1,0:T(8,128)(2,1)} %fusion.2.x_ref, bf16[128,1536]{1,0:T(8,128)(2,1)} %c_ref.1, ...), custom_call_target="tpu_custom_call" | custom-call | flops 14495514624 | bytes 18874368 | tf_op jit(solution)/shard_map/pallas_call | solution.py:360
  147.7 0.0 copy-start.2
  147.8 0.0 copy-start.3
  147.8 17.2 %fusion.14 = f32[1536,3072]{1,0:T(8,128)} fusion(bf16[1024,1536]{1,0:T(8,128)(2,1)} %bitcast.15, bf16[1024,3072]{1,0:T(8,128)(2,1)} %bitcast.13), kind=kOutput, calls=%fused_computation.23 | convolution fusion | flops 9663676416 | bytes 28311552 | tf_op jit(solution)/shard_map/dot_general | solution.py:405
  164.9 0.0 copy-done.2
  164.9 0.0 copy-done.3
  164.9 0.0 copy-start
  164.9 0.0 copy-start.1
  164.9 13.4 %fusion.15 = f32[3072,1536]{1,0:T(8,128)} fusion(bf16[1024,3072]{1,0:T(8,128)(2,1)S(1)} %bitcast.12, bf16[1024,1536]{1,0:T(8,128)(2,1)S(1)} %bitcast.14), kind=kOutput, calls=%fused_computation.24 | convolution fusion | flops 9663676416 | bytes 28311552 | tf_op jit(solution)/shard_map/dot_general | solution.py:401
  178.4 0.0 copy-done
  178.4 0.7 copy.12
  179.1 0.0 copy-done.1
  179.1 0.6 copy.13
  (2 shorter events, 0.0 us)
Async XLA Ops:
  147.7 17.2 %copy-start.2 = (bf16[8,4,32,3072]{3,2,1,0:T(8,128)(2,1)S(1)}, bf16[8,4,32,3072]{3,2,1,0:T(8,128)(2,1)}, u32[]{:S(2)}) copy-start(bf16[8,4,32,3072]{3,2,1,0:T(8,128)(2,1)} %get-tuple-element.14) | copy-start | bytes 18874372
  147.8 17.2 %copy-start.3 = (bf16[8,128,1536]{2,1,0:T(8,128)(2,1)S(1)}, bf16[8,128,1536]{2,1,0:T(8,128)(2,1)}, u32[]{:S(2)}) copy-start(bf16[8,128,1536]{2,1,0:T(8,128)(2,1)} %get-tuple-element.15) | copy-start | bytes 9437188
  164.9 13.5 %copy-start = (bf16[128,1536]{1,0:T(8,128)(2,1)S(1)}, bf16[128,1536]{1,0:T(8,128)(2,1)}, u32[]{:S(2)}) copy-start(bf16[128,1536]{1,0:T(8,128)(2,1)} %get-tuple-element.20) | copy-start | bytes 1179652
  164.9 14.2 %copy-start.1 = (f32[1,3072]{1,0:T(1,128)S(1)}, f32[1,3072]{1,0:T(1,128)}, u32[]{:S(2)}) copy-start(f32[1,3072]{1,0:T(1,128)} %get-tuple-element.13) | copy-start | bytes 36868
